TPU v7x, 512 devices: a whole 4x4x16 slice. The times are simulated.
512 devices in a mesh: dp: 32 (over x, y, core), tensor: 16 (over z).
Axes of the slice: x: 4, y: 4, z: 16, core: 2. Of those that a mesh axis runs over, the one named last changes fastest.
Arguments:
- tokens: bfloat16 [65536, 8192], P('dp', 'tensor'), may hold values from -6 to 6
- grad_out: bfloat16 [65536, 1024], P('dp', 'tensor'), may hold values from -0.14941406 to 0.14941406
- error_old: bfloat16 [32, 1024, 8192], P('dp', None, 'tensor'), may hold values from -3 to 3
- power_q: float32 [8192, 32], P('tensor'), may hold values from -6 to 6
Outputs:
- factor_q: float32 [8192, 32], P('tensor')
- error_new: bfloat16 [32, 1024, 8192], P('dp', None, 'tensor')
All inputs are finite; a program needn't handle non-finite values.
Results may differ from a plain program's by a relative error of at most 0.00045.
Values may be sent and summed in bfloat16 or wider, within the bound.
A program may use at most 64 MiB of HBM per device.

v0:
```python
import jax
import jax.numpy as jnp
from jax import lax
from jax.sharding import PartitionSpec as P


def local(tokens, grad_out, error_old, power_q):
    gradient = lax.dot_general(
        lax.all_gather(grad_out, "tensor", axis=1, tiled=True),
        tokens,
        (((0,), (0,)), ((), ())),
        preferred_element_type=jnp.float32,
    )
    merged = gradient + error_old[0].astype(jnp.float32)
    partial_p = jnp.dot(merged, power_q, precision=lax.Precision.HIGHEST)
    summed = lax.psum(partial_p, ("dp", "tensor"))
    gram_matrix = jnp.dot(summed.T, summed, precision=lax.Precision.HIGHEST)
    cholesky_factor = jnp.linalg.cholesky(gram_matrix)
    ortho_basis = lax.linalg.triangular_solve(
        cholesky_factor, summed, left_side=False, lower=True, transpose_a=True
    )
    local_q = lax.dot_general(
        merged,
        ortho_basis,
        (((0,), (0,)), ((), ())),
        precision=lax.Precision.HIGHEST,
        preferred_element_type=jnp.float32,
    )
    factor_q = lax.psum(local_q, "dp")
    low_rank = jnp.dot(ortho_basis, factor_q.T, precision=lax.Precision.HIGHEST) / lax.axis_size(
        "dp"
    )
    error_new = (merged - low_rank)[None].astype(jnp.bfloat16)
    return (factor_q, error_new)


def solution(mesh):
    placed = (P("dp", "tensor"), P("dp", "tensor"), P("dp", None, "tensor"), P("tensor", None))
    return jax.shard_map(
        local,
        mesh=mesh,
        in_specs=placed,
        out_specs=(P("tensor", None), P("dp", None, "tensor")),
        check_vma=False,
    )
```

profile of v0, /device:TPU:1, one launch (start us, length us, event | category | flops | bytes accessed | tf_op | source)
XLA Modules:
  0.0 689.6 jit_solution(4544617359959111940)
XLA Ops:
  7.2 0.0 copy-start
  7.2 0.0 all-gather.2.cloned.1.call-start
  7.2 0.7 all-gather.2.cloned.1.call-update
  7.9 0.0 copy-start.3
  7.9 0.0 all-reduce.3.cloned.1.call-start
  8.0 77.4 %all-gather.2.cloned.1.call-done = bf16[2048,1024]{0,1:T(8,128)(2,1)} async-done(((bf16[2048,64]{0,1:T(8,128)(2,1)}), bf16[2048,1024]{0,1:T(8,128)(2,1)}) %all-gather.2.cloned.1.call-update) | async-done | bytes 4194320 | tf_op jit(solution)/shard_map/all_gather | solution.py:9
  85.4 0.0 copy-done
  85.4 4.8 convert_add_fusion
  90.2 0.0 copy-start.1
  90.2 1.3 copy-done.1
  91.5 0.0 copy-done.3
  91.5 2.7 fusion.5
  94.2 0.0 all-reduce.3.cloned.1.call-update
  94.2 0.0 all-reduce.5.cloned.1.call-start
  94.3 454.1 %all-reduce.3.cloned.1.call-done = f32[1024,32]{0,1:T(8,128)} async-done(((f32[1024,32]{0,1:T(8,128)}), f32[1024,32]{0,1:T(8,128)}) %all-reduce.3.cloned.1.call-update) | async-done | bytes 131088 | tf_op jit(solution)/shard_map/psum | solution.py:16
  548.3 1.2 fusion.6
  549.5 0.1 copy.6
  549.6 2.9 cholesky.16
  552.6 0.6 compare_reduce_fusion
  553.2 0.7 fusion.1
  553.9 2.4 custom-call.6
  556.3 1.2 fusion.2
  557.6 3.6 fusion.7
  561.1 0.0 all-reduce.5.cloned.1.call-update
  561.1 116.8 %all-reduce.5.cloned.1.call-done = f32[512,32]{0,1:T(8,128)} async-done(((f32[512,32]{0,1:T(8,128)}), f32[512,32]{0,1:T(8,128)}) %all-reduce.5.cloned.1.call-update) | async-done | bytes 65552 | tf_op jit(solution)/shard_map/psum | solution.py:29
  677.9 0.0 copy-start.2
  677.9 4.5 fusion
  682.4 0.0 copy-done.2
  682.4 0.6 copy.9
  (2 shorter events, 0.0 us)
Async XLA Ops:
  7.2 78.2 %copy-start = (bf16[2048,512]{1,0:T(8,128)(2,1)S(1)}, bf16[2048,512]{1,0:T(8,128)(2,1)}, u32[]{:S(2)}) copy-start(bf16[2048,512]{1,0:T(8,128)(2,1)} %param.4) | copy-start | bytes 6291460
  7.2 78.2 %all-gather.2.cloned.1.call-start = ((), (), s32[]{:S(2)}) async-start(), calls=%async_computation | async-start | bytes 4456448 | tf_op jit(solution)/shard_map/all_gather | solution.py:9
  7.9 83.6 %copy-start.3 = (f32[512,32]{0,1:T(8,128)S(1)}, f32[512,32]{0,1:T(8,128)}, u32[]{:S(2)}) copy-start(f32[512,32]{0,1:T(8,128)} %param.7) | copy-start | bytes 196612
  7.9 540.4 %all-reduce.3.cloned.1.call-start = ((), (), s32[]{:S(2)}) async-start(), calls=%async_computation.1 | async-start | bytes 262144 | tf_op jit(solution)/shard_map/psum | solution.py:16
  90.2 1.3 copy-start.1
  94.2 583.7 %all-reduce.5.cloned.1.call-start = ((), (), s32[]{:S(2)}) async-start(), calls=%async_computation.2 | async-start | bytes 131072 | tf_op jit(solution)/shard_map/psum | solution.py:29
  677.9 4.5 copy-start.2
Sparse Core Ops, SparseCore 0:
  10.1 75.2 all-gather.1
  94.3 453.9 all-reduce.2
  561.3 116.5 all-reduce.4
where the time goes:
time: 690 us
  waiting for transfers between devices  649 us (94%)
  matrix products  18 us (3%)
  between operations  13.8 us (2%)
    psum x1, waiting for transfers between devices, local(): summed = lax.psum(partial_p, ('dp', 'tensor'))  454 us
    psum x1, waiting for transfers between devices, local(): factor_q = lax.psum(local_q, 'dp')  117 us
    all_gather x1, waiting for transfers between devices, local(): lax.all_gather(grad_out, 'tensor', axis=1, tiled=True)  77.4 us
  transfers between devices with their start and end apart: 3, of which 3 were waited for; matrix products, arithmetic and copies ran while one was open for 0% of the time, Pallas kernels for 0%

commit v1 on v0

v1 whole, which is shorter than its diff:
```python
import functools

import jax
import jax.numpy as jnp
from jax import lax
from jax.experimental import pallas as pl
from jax.experimental.pallas import tpu as pltpu
from jax.sharding import PartitionSpec as P

F32 = jnp.float32
BF16 = jnp.bfloat16
MESH = pl.DeviceIdType.MESH
HIGHEST = lax.Precision.HIGHEST
NT = (((1,), (1,)), ((), ()))
NN = (((1,), (0,)), ((), ()))
TN = (((0,), (0,)), ((), ()))
PIECES = 4


def split2(x):
    hi = x.astype(BF16)
    return hi, (x - hi.astype(F32)).astype(BF16)


def dot3(a, b, dims):
    a1, a2 = split2(a)
    b1, b2 = split2(b)
    dot = functools.partial(lax.dot_general, dimension_numbers=dims, preferred_element_type=F32)
    return dot(a1, b1) + (dot(a1, b2) + dot(a2, b1))


def kernel(
    nd, nz, gt_hbm, tok_hbm, err_hbm, qt_hbm, fq_hbm, new_hbm,
    gt, tok, err, qt, merged, out, fq,
    part_p, plane_p, deep_p, full_p, part_u, plane_u, full_u,
    load_sem, ring_send, ring_recv, send_sem, recv_sem, store_sem,
):
    dp = lax.axis_index("dp")
    z = lax.axis_index("tensor")
    hb = gt.shape[1]
    rows = hb // PIECES
    half = nz // 2
    rank = qt.shape[0]
    width = qt.shape[1]

    loads = [
        pltpu.make_async_copy(gt_hbm, gt.at[z], load_sem.at[0]),
        pltpu.make_async_copy(tok_hbm, tok, load_sem.at[1]),
        pltpu.make_async_copy(err_hbm, err, load_sem.at[2]),
        pltpu.make_async_copy(qt_hbm, qt, load_sem.at[3]),
    ]
    for load in loads:
        load.start()

    barrier = pltpu.get_barrier_semaphore()

    def greet(axis, n, me):
        def body(k, carry):
            pl.semaphore_signal(
                barrier, inc=1, device_id={axis: lax.rem(me + k, n)}, device_id_type=MESH
            )
            return carry

        lax.fori_loop(1, n, body, 0)

    greet("tensor", nz, z)
    greet("dp", nd, dp)
    pl.semaphore_wait(barrier, nd + nz - 2)

    def ring(way, step, piece):
        sign = 1 if way == 0 else -1
        block = lax.rem(z - sign * step + 2 * nz, nz)
        there = lax.rem(z + sign + nz, nz)
        ref = gt.at[block, pl.ds(piece * rows, rows)]
        return pltpu.make_async_remote_copy(
            src_ref=ref,
            dst_ref=ref,
            send_sem=ring_send.at[way, step, piece],
            recv_sem=ring_recv.at[way, step, piece],
            device_id={"tensor": there},
            device_id_type=MESH,
        )

    def arrived(way, step, piece):
        sign = 1 if way == 0 else -1
        block = lax.rem(z - sign * (step + 1) + 2 * nz, nz)
        ref = gt.at[block, pl.ds(piece * rows, rows)]
        pltpu.make_async_copy(ref, ref, ring_recv.at[way, step, piece]).wait()

    def multiply(block_a, block_b=None):
        x = gt[block_a]
        if block_b is not None:
            x = jnp.concatenate([x, gt[block_b]], axis=0)
        y = jnp.dot(x, tok[...], preferred_element_type=F32)
        merged[block_a] = y[:hb] + err[block_a].astype(F32)
        if block_b is not None:
            merged[block_b] = y[hb:] + err[block_b].astype(F32)

    loads[0].wait()
    for piece in range(PIECES):
        ring(0, 0, piece).start()
        ring(1, 0, piece).start()
    for load in loads[1:]:
        load.wait()
    multiply(z)

    def step_body(s, carry):
        for piece in range(PIECES):
            for way in range(2):
                arrived(way, s - 1, piece)
                ring(way, s, piece).start()
        multiply(lax.rem(z + s, nz), lax.rem(z - s + nz, nz))
        return carry

    lax.fori_loop(1, half - 1, step_body, 0)
    s = half - 1
    for piece in range(PIECES):
        for way in range(2):
            arrived(way, s - 1, piece)
            if (piece < PIECES // 2) == (way == 0):
                ring(way, s, piece).start()
    multiply(lax.rem(z + s, nz), lax.rem(z - s + nz, nz))
    for piece in range(PIECES):
        arrived(0 if piece < PIECES // 2 else 1, s, piece)
    multiply(lax.rem(z + half, nz))

    hd = nz * hb
    part = dot3(qt[...], merged[...].reshape(hd, width), NT)

    def exchange(axis, n, me, sems, source, target):
        def one(k):
            there = lax.rem(me + k, n)
            return pltpu.make_async_remote_copy(
                src_ref=source(there),
                dst_ref=target.at[me],
                send_sem=send_sem.at[sems],
                recv_sem=recv_sem.at[sems],
                device_id={axis: there},
                device_id_type=MESH,
            )

        def body(k, carry):
            one(k).start()
            return carry

        lax.fori_loop(1, n, body, 0)

    def landed(sems, n, target):
        rest = target.at[pl.ds(0, n - 1)]
        pltpu.make_async_copy(rest, rest, recv_sem.at[sems]).wait()

    def left(sems, n, target):
        rest = target.at[pl.ds(0, n - 1)]
        pltpu.make_async_copy(rest, rest, send_sem.at[sems]).wait()

    tiles = hd // 128
    for i in range(rank // 8):
        for j in range(tiles):
            part_p[i * tiles + j] = part[i * 8 : i * 8 + 8, j * 128 : j * 128 + 128]
    plane_p[dp] = part_p[dp]
    exchange("dp", nd, dp, 0, lambda there: part_p.at[there], plane_p)
    landed(0, nd, plane_p)
    deep_p[z] = jnp.sum(plane_p[...], axis=0)
    exchange("tensor", nz, z, 1, lambda there: deep_p.at[z], deep_p)
    landed(1, nz, deep_p)
    full_p[dp] = jnp.sum(deep_p[...], axis=0)
    exchange("dp", nd, dp, 2, lambda there: full_p.at[dp], full_p)
    landed(2, nd, full_p)
    pt = jnp.concatenate(
        [
            jnp.concatenate([full_p[i * tiles + j] for j in range(tiles)], axis=1)
            for i in range(rank // 8)
        ],
        axis=0,
    )

    ut = dot3(pt, merged[...].reshape(hd, width), NN)
    urows = part_u.shape[1]
    utiles = width // 128
    for i in range(rank // urows):
        for j in range(utiles):
            part_u[i * utiles + j] = ut[i * urows : (i + 1) * urows, j * 128 : j * 128 + 128]
    plane_u[dp] = part_u[dp]
    exchange("dp", nd, dp, 3, lambda there: part_u.at[there], plane_u)

    gram = lax.dot_general(pt, pt, NT, precision=HIGHEST, preferred_element_type=F32)
    row_id = lax.broadcasted_iota(jnp.int32, (rank, 1), 0)
    eye = (
        lax.broadcasted_iota(jnp.int32, (rank, rank), 0)
        == lax.broadcasted_iota(jnp.int32, (rank, rank), 1)
    ).astype(F32)
    x = jnp.concatenate([gram, eye], axis=1)

    def eliminate(x, start, stop):
        for k in range(start, stop):
            d = x[k : k + 1, k : k + 1]
            r = lax.rsqrt(d)
            r = r * (1.5 - 0.5 * d * r * r)
            row = x[k : k + 1, :] * r
            column = x[:, k : k + 1] * r
            x = jnp.where(row_id == k, row, jnp.where(row_id > k, x - column * row, x))
        return x

    x = eliminate(x, 0, rank // 2)
    landed(3, nd, plane_u)
    full_u[dp] = jnp.sum(plane_u[...], axis=0)
    exchange("dp", nd, dp, 4, lambda there: full_u.at[dp], full_u)
    x = eliminate(x, rank // 2, rank)
    inverse = x[:, rank:]
    landed(4, nd, full_u)
    ut = jnp.concatenate(
        [
            jnp.concatenate([full_u[i * utiles + j] for j in range(utiles)], axis=1)
            for i in range(rank // urows)
        ],
        axis=0,
    )
    fqt = lax.dot_general(inverse, ut, NN, precision=HIGHEST, preferred_element_type=F32)
    fq[...] = fqt
    fq_store = pltpu.make_async_copy(fq, fq_hbm, store_sem.at[0])
    fq_store.start()
    mix = lax.dot_general(inverse, fqt, TN, precision=HIGHEST, preferred_element_type=F32) / nd
    p1, p2 = split2(pt)
    m1, m2 = split2(mix)
    left_side = jnp.concatenate([p1, p1, p2], axis=0)
    right_side = jnp.concatenate([m1, m2, m1], axis=0)
    stores = []
    groups = 4
    per = nz // groups
    for g in range(groups):
        n = per * hb
        low = lax.dot_general(
            left_side[:, g * n : (g + 1) * n], right_side, TN, preferred_element_type=F32
        )
        at = pl.ds(g * per, per)
        out[at] = (merged[at] - low.reshape(per, hb, width)).astype(BF16)
        store = pltpu.make_async_copy(out.at[at], new_hbm.at[at], store_sem.at[1 + g])
        store.start()
        stores.append(store)

    def sent(s, carry):
        for piece in range(PIECES):
            for way in range(2):
                ring(way, s, piece).wait_send()
        return carry

    lax.fori_loop(0, half - 1, sent, 0)
    for piece in range(PIECES):
        ring(0 if piece < PIECES // 2 else 1, half - 1, piece).wait_send()
    left(0, nd, plane_p)
    left(1, nz, deep_p)
    left(2, nd, full_p)
    left(3, nd, plane_u)
    left(4, nd, full_u)
    fq_store.wait()
    for store in stores:
        store.wait()


def local(nd, nz, tokens, grad_out, error_old, power_q):
    tok_n, hb = grad_out.shape
    width = tokens.shape[1]
    rank = power_q.shape[1]
    hd = hb * nz
    chunk = rank * hd // nd // 128
    urows = rank * width // nd // 128
    any_space = pl.BlockSpec(memory_space=pl.ANY)
    fqt, new = pl.pallas_call(
        functools.partial(kernel, nd, nz),
        out_shape=(
            jax.ShapeDtypeStruct((rank, width), F32),
            jax.ShapeDtypeStruct((nz, hb, width), BF16),
        ),
        in_specs=[any_space] * 4,
        out_specs=(any_space, any_space),
        scratch_shapes=[
            pltpu.VMEM((nz, hb, tok_n), BF16),
            pltpu.VMEM((tok_n, width), BF16),
            pltpu.VMEM((nz, hb, width), BF16),
            pltpu.VMEM((rank, width), F32),
            pltpu.VMEM((nz, hb, width), F32),
            pltpu.VMEM((nz, hb, width), BF16),
            pltpu.VMEM((rank, width), F32),
            pltpu.VMEM((nd, chunk, 128), F32),
            pltpu.VMEM((nd, chunk, 128), F32),
            pltpu.VMEM((nz, chunk, 128), F32),
            pltpu.VMEM((nd, chunk, 128), F32),
            pltpu.VMEM((nd, urows, 128), F32),
            pltpu.VMEM((nd, urows, 128), F32),
            pltpu.VMEM((nd, urows, 128), F32),
            pltpu.SemaphoreType.DMA((4,)),
            pltpu.SemaphoreType.DMA((2, nz // 2, PIECES)),
            pltpu.SemaphoreType.DMA((2, nz // 2, PIECES)),
            pltpu.SemaphoreType.DMA((5,)),
            pltpu.SemaphoreType.DMA((5,)),
            pltpu.SemaphoreType.DMA((5,)),
        ],
        compiler_params=pltpu.CompilerParams(
            collective_id=0, has_side_effects=True, vmem_limit_bytes=48 * 1024 * 1024
        ),
    )(grad_out.T, tokens, error_old.reshape(nz, hb, width), power_q.T)
    return fqt.T, new.reshape(1, hd, width)


def solution(mesh):
    placed = (P("dp", "tensor"), P("dp", "tensor"), P("dp", None, "tensor"), P("tensor", None))
    return jax.shard_map(
        functools.partial(local, mesh.shape["dp"], mesh.shape["tensor"]),
        mesh=mesh,
        in_specs=placed,
        out_specs=(P("tensor", None), P("dp", None, "tensor")),
        check_vma=False,
    )
```

time: 690 us -> 102 us (0.15)
  waiting for transfers between devices: 649 us -> 0 us
  Pallas kernels: 0 us -> 95.1 us
  matrix products: 18 us -> 0 us
  between operations: 13.8 us -> 0.65 us
    psum x2 -> x0, waiting for transfers between devices: 571 us -> none  [the longest x1 454 us: local(): summed = lax.psum(partial_p, ('dp', 'tensor'))]
    pallas_call x0 -> x1, Pallas kernels: none -> 95.1 us  [local(): pl.pallas_call(functools.partial(kernel, nd, nz), out_shape=(jax.ShapeDty...]
    all_gather x1 -> x0, waiting for transfers between devices: 77.4 us -> none  [local(): lax.all_gather(grad_out, 'tensor', axis=1, tiled=True)]
    dot_general x5 -> x0, matrix products: 16.8 us -> none  [the longest x1 4.8 us: local(): lax.dot_general(lax.all_gather(grad_out, 'tensor', axis=1, tiled=True), t...]
  transfers between devices with their start and end apart: 3 -> 0, of which waited for: 3 -> 0; matrix products, arithmetic and copies ran while one was open for 0% -> 0% of each run, Pallas kernels for 0% -> 0%
where the time goes in v1:
time: 102 us
  Pallas kernels  95.1 us (93%)
  local copies, waits for them, and re-layouts  6.2 us (6%)
    pallas_call x1, Pallas kernels, local(): pl.pallas_call(functools.partial(kernel, nd, nz), out_shape=(jax.ShapeDty...  95.1 us
    unnamed x10, local copies, waits for them, and re-layouts  6.2 us

profile of v1, /device:TPU:1, one launch (start us, length us, event | category | flops | bytes accessed | tf_op | source)
XLA Modules:
  0.0 102.0 jit_solution(3861968364717443842)
XLA Ops:
  0.6 0.0 copy-start
  0.6 1.6 %copy-done = bf16[2048,512]{1,0:T(8,128)(2,1)S(1)} copy-done((bf16[2048,512]{1,0:T(8,128)(2,1)S(1)}, bf16[2048,512]{1,0:T(8,128)(2,1)}, u32[]{:S(2)}) %copy-start) | copy-done | bytes 2097176
  2.2 0.0 copy-start.1
  2.2 1.2 %copy-done.1 = bf16[1,1024,512]{2,1,0:T(8,128)(2,1)S(1)} copy-done((bf16[1,1024,512]{2,1,0:T(8,128)(2,1)S(1)}, bf16[1,1024,512]{2,1,0:T(8,128)(2,1)}, u32[]{:S(2)}) %copy-start.1) | copy-done | bytes 1048600
  3.4 0.0 copy-start.2
  3.5 0.9 copy-done.2
  4.4 0.0 copy-start.3
  4.4 0.8 copy-done.3
  5.2 95.1 %shard_map.59 = (f32[32,512]{1,0:T(8,128)S(1)}, bf16[16,64,512]{2,1,0:T(8,128)(2,1)S(1)}) custom-call(bf16[64,2048]{1,0:T(8,128)(2,1)S(1)} %bitcast.7, bf16[2048,512]{1,0:T(8,128)(2,1)S(1)} %copy-done, bf16[16,64,512]{2,1,0:T(8,128)(2,1)S(1)} %bitcast.5, f32[32,512]{1,0:T(8,128)S(1)} %bitcast.8), custom_call_target="tpu_custom_call" | custom-call | tf_op jit(solution)/shard_map/pallas_call | solution.py:268
  100.4 0.6 copy.8
  101.0 1.0 copy.9
Async XLA Ops:
  0.6 1.6 %copy-start = (bf16[2048,512]{1,0:T(8,128)(2,1)S(1)}, bf16[2048,512]{1,0:T(8,128)(2,1)}, u32[]{:S(2)}) copy-start(bf16[2048,512]{1,0:T(8,128)(2,1)} %tok_hbm.1) | copy-start | bytes 6291460
  2.2 1.2 %copy-start.1 = (bf16[1,1024,512]{2,1,0:T(8,128)(2,1)S(1)}, bf16[1,1024,512]{2,1,0:T(8,128)(2,1)}, u32[]{:S(2)}) copy-start(bf16[1,1024,512]{2,1,0:T(8,128)(2,1)} %param.6) | copy-start | bytes 3145732
  3.4 0.9 copy-start.2
  4.4 0.8 copy-start.3

commit v2 on v1

--- a/solution.py
+++ b/solution.py
@@ -63,9 +63,12 @@
 
         lax.fori_loop(1, n, body, 0)
 
-    greet("tensor", nz, z)
+    for step in (1, nz - 1):
+        pl.semaphore_signal(
+            barrier, inc=1, device_id={"tensor": lax.rem(z + step, nz)}, device_id_type=MESH
+        )
     greet("dp", nd, dp)
-    pl.semaphore_wait(barrier, nd + nz - 2)
+    pl.semaphore_wait(barrier, nd + 1)
 
     def ring(way, step, piece):
         sign = 1 if way == 0 else -1
@@ -264,6 +267,7 @@
     hd = hb * nz
     chunk = rank * hd // nd // 128
     urows = rank * width // nd // 128
+    operands = (grad_out.T, tokens, error_old.reshape(nz, hb, width), power_q.T)
     any_space = pl.BlockSpec(memory_space=pl.ANY)
     fqt, new = pl.pallas_call(
         functools.partial(kernel, nd, nz),
@@ -298,7 +302,7 @@
         compiler_params=pltpu.CompilerParams(
             collective_id=0, has_side_effects=True, vmem_limit_bytes=48 * 1024 * 1024
         ),
-    )(grad_out.T, tokens, error_old.reshape(nz, hb, width), power_q.T)
+    )(*(pltpu.with_memory_space_constraint(a, pltpu.HBM) for a in operands))
     return fqt.T, new.reshape(1, hd, width)
 
 

time: 102 us -> 96.4 us (0.945)
  local copies, waits for them, and re-layouts: 6.2 us -> 1.6 us
  Pallas kernels: 95.1 us -> 94 us
    unnamed x10 -> x2, local copies, waits for them, and re-layouts: 6.2 us -> 1.6 us
    pallas_call x1, Pallas kernels: 95.1 us -> 94 us  [local(): pl.pallas_call(functools.partial(kernel, nd, nz), out_shape=(jax.ShapeDty...]
where the time goes in v2:
time: 96.4 us; the launch traced here: 96.3 us
  Pallas kernels  94 us (98%)
  local copies, waits for them, and re-layouts  1.6 us (2%)
    pallas_call x1, Pallas kernels, local(): pl.pallas_call(functools.partial(kernel, nd, nz), out_shape=(jax.ShapeDty...  94 us

profile of v2, /device:TPU:1, one launch (start us, length us, event | category | flops | bytes accessed | tf_op | source)
XLA Modules:
  0.0 96.3 jit_solution(12111799528792443935)
XLA Ops:
  0.6 94.0 %shard_map.59 = (f32[32,512]{1,0:T(8,128)S(1)}, bf16[16,64,512]{2,1,0:T(8,128)(2,1)S(1)}) custom-call(bf16[64,2048]{1,0:T(8,128)(2,1)} %bitcast.8, bf16[2048,512]{1,0:T(8,128)(2,1)} %tok_hbm.1, bf16[16,64,512]{2,1,0:T(8,128)(2,1)} %bitcast.7, f32[32,512]{1,0:T(8,128)} %bitcast.9), custom_call_target="tpu_custom_call" | custom-call | tf_op jit(solution)/shard_map/pallas_call | solution.py:272
  94.7 0.6 copy.8
  95.3 1.0 %copy.9 = bf16[1,1024,512]{2,1,0:T(8,128)(2,1)} copy(bf16[1,1024,512]{2,1,0:T(8,128)(2,1)S(1)} %bitcast.5) | data formatting | bytes 2097152

commit v3 on v2

--- a/solution.py
+++ b/solution.py
@@ -1,4 +1,5 @@
 import functools
+import math
 
 import jax
 import jax.numpy as jnp
@@ -15,6 +16,7 @@
 NN = (((1,), (0,)), ((), ()))
 TN = (((0,), (0,)), ((), ()))
 PIECES = 4
+BATCHES = 8
 
 
 def split2(x):
@@ -32,7 +34,8 @@
 def kernel(
     nd, nz, gt_hbm, tok_hbm, err_hbm, qt_hbm, fq_hbm, new_hbm,
     gt, tok, err, qt, merged, out, fq,
-    part_p, plane_p, deep_p, full_p, part_u, plane_u, full_u,
+    stage, plane_m, total_m, late_stage, late_plane, deep_p, full_p, natural_p,
+    part_u, plane_u, full_u,
     load_sem, ring_send, ring_recv, send_sem, recv_sem, store_sem,
 ):
     dp = lax.axis_index("dp")
@@ -40,8 +43,13 @@
     hb = gt.shape[1]
     rows = hb // PIECES
     half = nz // 2
-    rank = qt.shape[0]
-    width = qt.shape[1]
+    rank, width = qt.shape
+    q = qt
+    own = hb // nd
+    across = math.isqrt(nd // 2)
+    place = (dp // (2 * across), lax.rem(dp // 2, across), lax.rem(dp, 2))
+    offsets = [(i, j, k) for i in range(across) for j in range(across) for k in range(2)][1:]
+    far_first = sorted(offsets, key=lambda o: -sum(min(v, across - v) for v in o[:2]))
 
     loads = [
         pltpu.make_async_copy(gt_hbm, gt.at[z], load_sem.at[0]),
@@ -90,14 +98,95 @@
         ref = gt.at[block, pl.ds(piece * rows, rows)]
         pltpu.make_async_copy(ref, ref, ring_recv.at[way, step, piece]).wait()
 
-    def multiply(block_a, block_b=None):
-        x = gt[block_a]
-        if block_b is not None:
-            x = jnp.concatenate([x, gt[block_b]], axis=0)
+    def exchange_dp(sems, source, target):
+        for offset in far_first:
+            there = (
+                lax.rem(place[0] + offset[0], across) * across
+                + lax.rem(place[1] + offset[1], across)
+            ) * 2 + lax.rem(place[2] + offset[2], 2)
+            pltpu.make_async_remote_copy(
+                src_ref=source(there),
+                dst_ref=target.at[dp],
+                send_sem=send_sem.at[sems],
+                recv_sem=recv_sem.at[sems],
+                device_id={"dp": there},
+                device_id_type=MESH,
+            ).start()
+
+    def exchange_z(sems, source, target):
+        for offset in sorted(range(1, nz), key=lambda k: -min(k, nz - k)):
+            pltpu.make_async_remote_copy(
+                src_ref=source,
+                dst_ref=target.at[z],
+                send_sem=send_sem.at[sems],
+                recv_sem=recv_sem.at[sems],
+                device_id={"tensor": lax.rem(z + offset, nz)},
+                device_id_type=MESH,
+            ).start()
+
+    def landed(sems, n, target):
+        rest = target.at[pl.ds(0, n - 1)]
+        pltpu.make_async_copy(rest, rest, recv_sem.at[sems]).wait()
+
+    def left(sems, n, target):
+        rest = target.at[pl.ds(0, n - 1)]
+        pltpu.make_async_copy(rest, rest, send_sem.at[sems]).wait()
+
+    def at(offset):
+        return lax.rem(z + offset + 2 * nz, nz)
+
+    def multiply(*blocks):
+        x = [gt[block] for block in blocks]
+        x = x[0] if len(x) == 1 else jnp.concatenate(x, axis=0)
         y = jnp.dot(x, tok[...], preferred_element_type=F32)
-        merged[block_a] = y[:hb] + err[block_a].astype(F32)
-        if block_b is not None:
-            merged[block_b] = y[hb:] + err[block_b].astype(F32)
+        parts = []
+        for i, block in enumerate(blocks):
+            part = y[i * hb : (i + 1) * hb] + err[block].astype(F32)
+            merged[block] = part
+            parts.append(part.reshape(nd, own, width))
+        return parts
+
+    def batch_of(step):
+        return step * BATCHES // half
+
+    slots = {}
+    for step in range(half):
+        for block in ((0,) if step == 0 else (step, -step)):
+            batch = batch_of(step)
+            slots[block] = (batch, sum(1 for b in slots.values() if b[0] == batch))
+    counts = [sum(1 for b in slots.values() if b[0] == k) for k in range(BATCHES)]
+    starts = [sum(counts[:k]) for k in range(BATCHES)]
+
+    def put(step):
+        blocks = (0,) if step == 0 else (step, -step)
+        for block, part in zip(blocks, multiply(*(at(b) for b in blocks)), strict=True):
+            batch, slot = slots[block]
+            stage[:, starts[batch] + slot] = part
+        batch = batch_of(step)
+        if step == half - 1 or batch_of(step + 1) != batch:
+            span = pl.ds(starts[batch], counts[batch])
+            plane_m[dp, span] = stage[dp, span]
+            for offset in far_first:
+                there = (
+                    lax.rem(place[0] + offset[0], across) * across
+                    + lax.rem(place[1] + offset[1], across)
+                ) * 2 + lax.rem(place[2] + offset[2], 2)
+                pltpu.make_async_remote_copy(
+                    src_ref=stage.at[there, span],
+                    dst_ref=plane_m.at[dp, span],
+                    send_sem=send_sem.at[5 + batch],
+                    recv_sem=recv_sem.at[5 + batch],
+                    device_id={"dp": there},
+                    device_id_type=MESH,
+                ).start()
+
+    def gather_batch(batch):
+        span = pl.ds(starts[batch], counts[batch])
+        rest = plane_m.at[pl.ds(0, nd - 1), span]
+        pltpu.make_async_copy(rest, rest, recv_sem.at[5 + batch]).wait()
+        for block, (b, slot) in slots.items():
+            if b == batch:
+                total_m[at(block)] = jnp.sum(plane_m[:, starts[b] + slot], axis=0)
 
     loads[0].wait()
     for piece in range(PIECES):
@@ -105,88 +194,57 @@
         ring(1, 0, piece).start()
     for load in loads[1:]:
         load.wait()
-    multiply(z)
-
-    def step_body(s, carry):
+    put(0)
+    for s in range(1, half):
         for piece in range(PIECES):
             for way in range(2):
                 arrived(way, s - 1, piece)
-                ring(way, s, piece).start()
-        multiply(lax.rem(z + s, nz), lax.rem(z - s + nz, nz))
-        return carry
-
-    lax.fori_loop(1, half - 1, step_body, 0)
-    s = half - 1
+                if s < half - 1 or (piece < PIECES // 2) == (way == 0):
+                    ring(way, s, piece).start()
+        put(s)
+        if s < half - 1 and batch_of(s + 1) != batch_of(s) and batch_of(s) > 0:
+            gather_batch(batch_of(s) - 1)
+    gather_batch(BATCHES - 2)
     for piece in range(PIECES):
-        for way in range(2):
-            arrived(way, s - 1, piece)
-            if (piece < PIECES // 2) == (way == 0):
-                ring(way, s, piece).start()
-    multiply(lax.rem(z + s, nz), lax.rem(z - s + nz, nz))
-    for piece in range(PIECES):
-        arrived(0 if piece < PIECES // 2 else 1, s, piece)
-    multiply(lax.rem(z + half, nz))
+        arrived(0 if piece < PIECES // 2 else 1, half - 1, piece)
+    late_stage[...] = multiply(at(half))[0]
+    late_plane[dp] = late_stage[dp]
+    exchange_dp(0, lambda there: late_stage.at[there], late_plane)
+    gather_batch(BATCHES - 1)
+    landed(0, nd, late_plane)
+    total_m[at(half)] = jnp.sum(late_plane[...], axis=0)
 
     hd = nz * hb
-    part = dot3(qt[...], merged[...].reshape(hd, width), NT)
-
-    def exchange(axis, n, me, sems, source, target):
-        def one(k):
-            there = lax.rem(me + k, n)
-            return pltpu.make_async_remote_copy(
-                src_ref=source(there),
-                dst_ref=target.at[me],
-                send_sem=send_sem.at[sems],
-                recv_sem=recv_sem.at[sems],
-                device_id={axis: there},
-                device_id_type=MESH,
-            )
-
-        def body(k, carry):
-            one(k).start()
-            return carry
-
-        lax.fori_loop(1, n, body, 0)
-
-    def landed(sems, n, target):
-        rest = target.at[pl.ds(0, n - 1)]
-        pltpu.make_async_copy(rest, rest, recv_sem.at[sems]).wait()
-
-    def left(sems, n, target):
-        rest = target.at[pl.ds(0, n - 1)]
-        pltpu.make_async_copy(rest, rest, send_sem.at[sems]).wait()
-
-    tiles = hd // 128
-    for i in range(rank // 8):
-        for j in range(tiles):
-            part_p[i * tiles + j] = part[i * 8 : i * 8 + 8, j * 128 : j * 128 + 128]
-    plane_p[dp] = part_p[dp]
-    exchange("dp", nd, dp, 0, lambda there: part_p.at[there], plane_p)
-    landed(0, nd, plane_p)
-    deep_p[z] = jnp.sum(plane_p[...], axis=0)
-    exchange("tensor", nz, z, 1, lambda there: deep_p.at[z], deep_p)
+    rows_p = nz * own
+    m = total_m[...].reshape(rows_p, width)
+    part = dot3(m, q[...], NT)
+    groups = 128 // rank
+    high = rows_p // groups
+    deep_p[z] = jnp.concatenate([part[k * high : (k + 1) * high] for k in range(groups)], axis=1)
+    exchange_z(1, deep_p.at[z], deep_p)
     landed(1, nz, deep_p)
-    full_p[dp] = jnp.sum(deep_p[...], axis=0)
-    exchange("dp", nd, dp, 2, lambda there: full_p.at[dp], full_p)
-    landed(2, nd, full_p)
-    pt = jnp.concatenate(
-        [
-            jnp.concatenate([full_p[i * tiles + j] for j in range(tiles)], axis=1)
-            for i in range(rank // 8)
-        ],
-        axis=0,
-    )
-
-    ut = dot3(pt, merged[...].reshape(hd, width), NN)
+    packed = jnp.sum(deep_p[...], axis=0)
+
+    def unpack(x):
+        return jnp.concatenate([x[:, k * rank : (k + 1) * rank] for k in range(groups)], axis=0)
+
+    full_p[dp] = packed
+    exchange_dp(2, lambda there: full_p.at[dp], full_p)
+
+    ut = dot3(unpack(packed), m, TN)
     urows = part_u.shape[1]
     utiles = width // 128
     for i in range(rank // urows):
         for j in range(utiles):
             part_u[i * utiles + j] = ut[i * urows : (i + 1) * urows, j * 128 : j * 128 + 128]
     plane_u[dp] = part_u[dp]
-    exchange("dp", nd, dp, 3, lambda there: part_u.at[there], plane_u)
-
-    gram = lax.dot_general(pt, pt, NT, precision=HIGHEST, preferred_element_type=F32)
+    exchange_dp(3, lambda there: part_u.at[there], plane_u)
+    landed(2, nd, full_p)
+    for j in range(nd):
+        natural_p[:, j * own : (j + 1) * own] = unpack(full_p[j]).reshape(nz, own, rank)
+    p = natural_p[...].reshape(hd, rank)
+
+    gram = lax.dot_general(p, p, TN, precision=HIGHEST, preferred_element_type=F32)
     row_id = lax.broadcasted_iota(jnp.int32, (rank, 1), 0)
     eye = (
         lax.broadcasted_iota(jnp.int32, (rank, rank), 0)
@@ -204,11 +262,10 @@
             x = jnp.where(row_id == k, row, jnp.where(row_id > k, x - column * row, x))
         return x
 
-    x = eliminate(x, 0, rank // 2)
     landed(3, nd, plane_u)
     full_u[dp] = jnp.sum(plane_u[...], axis=0)
-    exchange("dp", nd, dp, 4, lambda there: full_u.at[dp], full_u)
-    x = eliminate(x, rank // 2, rank)
+    exchange_dp(4, lambda there: full_u.at[dp], full_u)
+    x = eliminate(x, 0, rank)
     inverse = x[:, rank:]
     landed(4, nd, full_u)
     ut = jnp.concatenate(
@@ -223,17 +280,17 @@
     fq_store = pltpu.make_async_copy(fq, fq_hbm, store_sem.at[0])
     fq_store.start()
     mix = lax.dot_general(inverse, fqt, TN, precision=HIGHEST, preferred_element_type=F32) / nd
-    p1, p2 = split2(pt)
+    p1, p2 = split2(p)
     m1, m2 = split2(mix)
-    left_side = jnp.concatenate([p1, p1, p2], axis=0)
+    left_side = jnp.concatenate([p1, p1, p2], axis=1)
     right_side = jnp.concatenate([m1, m2, m1], axis=0)
     stores = []
-    groups = 4
-    per = nz // groups
-    for g in range(groups):
+    parts = 4
+    per = nz // parts
+    for g in range(parts):
         n = per * hb
         low = lax.dot_general(
-            left_side[:, g * n : (g + 1) * n], right_side, TN, preferred_element_type=F32
+            left_side[g * n : (g + 1) * n], right_side, NN, preferred_element_type=F32
         )
         at = pl.ds(g * per, per)
         out[at] = (merged[at] - low.reshape(per, hb, width)).astype(BF16)
@@ -250,7 +307,10 @@
     lax.fori_loop(0, half - 1, sent, 0)
     for piece in range(PIECES):
         ring(0 if piece < PIECES // 2 else 1, half - 1, piece).wait_send()
-    left(0, nd, plane_p)
+    for batch in range(BATCHES):
+        rest = plane_m.at[pl.ds(0, nd - 1), pl.ds(starts[batch], counts[batch])]
+        pltpu.make_async_copy(rest, rest, send_sem.at[5 + batch]).wait()
+    left(0, nd, late_plane)
     left(1, nz, deep_p)
     left(2, nd, full_p)
     left(3, nd, plane_u)
@@ -285,18 +345,22 @@
             pltpu.VMEM((nz, hb, width), F32),
             pltpu.VMEM((nz, hb, width), BF16),
             pltpu.VMEM((rank, width), F32),
-            pltpu.VMEM((nd, chunk, 128), F32),
-            pltpu.VMEM((nd, chunk, 128), F32),
+            pltpu.VMEM((nd, nz - 1, hb // nd, width), F32),
+            pltpu.VMEM((nd, nz - 1, hb // nd, width), F32),
+            pltpu.VMEM((nz, hb // nd, width), F32),
+            pltpu.VMEM((nd, hb // nd, width), F32),
+            pltpu.VMEM((nd, hb // nd, width), F32),
             pltpu.VMEM((nz, chunk, 128), F32),
             pltpu.VMEM((nd, chunk, 128), F32),
+            pltpu.VMEM((nz, hb, rank), F32),
             pltpu.VMEM((nd, urows, 128), F32),
             pltpu.VMEM((nd, urows, 128), F32),
             pltpu.VMEM((nd, urows, 128), F32),
             pltpu.SemaphoreType.DMA((4,)),
             pltpu.SemaphoreType.DMA((2, nz // 2, PIECES)),
             pltpu.SemaphoreType.DMA((2, nz // 2, PIECES)),
-            pltpu.SemaphoreType.DMA((5,)),
-            pltpu.SemaphoreType.DMA((5,)),
+            pltpu.SemaphoreType.DMA((5 + BATCHES,)),
+            pltpu.SemaphoreType.DMA((5 + BATCHES,)),
             pltpu.SemaphoreType.DMA((5,)),
         ],
         compiler_params=pltpu.CompilerParams(

time: 96.4 us -> 91.8 us (0.952)
  Pallas kernels: 94 us -> 89.4 us
    pallas_call x1, Pallas kernels: 94 us -> 89.4 us  [local(): pl.pallas_call(functools.partial(kernel, nd, nz), out_shape=(jax.ShapeDty...]
where the time goes in v3:
time: 91.8 us; the launch traced here: 91.7 us
  Pallas kernels  89.4 us (97%)
  local copies, waits for them, and re-layouts  1.6 us (2%)
    pallas_call x1, Pallas kernels, local(): pl.pallas_call(functools.partial(kernel, nd, nz), out_shape=(jax.ShapeDty...  89.4 us

profile of v3, /device:TPU:1, one launch (start us, length us, event | category | flops | bytes accessed | tf_op | source)
XLA Modules:
  0.0 91.7 jit_solution(12086407229778902386)
XLA Ops:
  0.6 89.4 %shard_map.59 = (f32[32,512]{1,0:T(8,128)S(1)}, bf16[16,64,512]{2,1,0:T(8,128)(2,1)S(1)}) custom-call(bf16[64,2048]{1,0:T(8,128)(2,1)} %bitcast.8, bf16[2048,512]{1,0:T(8,128)(2,1)} %tok_hbm.1, bf16[16,64,512]{2,1,0:T(8,128)(2,1)} %bitcast.7, f32[32,512]{1,0:T(8,128)} %bitcast.9), custom_call_target="tpu_custom_call" | custom-call | tf_op jit(solution)/shard_map/pallas_call | solution.py:332
  90.1 0.6 copy.8
  90.7 1.0 %copy.9 = bf16[1,1024,512]{2,1,0:T(8,128)(2,1)} copy(bf16[1,1024,512]{2,1,0:T(8,128)(2,1)S(1)} %bitcast.5) | data formatting | bytes 2097152

commit v4 on v3

--- a/solution.py
+++ b/solution.py
@@ -12,11 +12,11 @@
 BF16 = jnp.bfloat16
 MESH = pl.DeviceIdType.MESH
 HIGHEST = lax.Precision.HIGHEST
+GROUPS = 4
 NT = (((1,), (1,)), ((), ()))
 NN = (((1,), (0,)), ((), ()))
 TN = (((0,), (0,)), ((), ()))
 PIECES = 4
-BATCHES = 8
 
 
 def split2(x):
@@ -32,11 +32,11 @@
 
 
 def kernel(
-    nd, nz, gt_hbm, tok_hbm, err_hbm, qt_hbm, fq_hbm, new_hbm,
-    gt, tok, err, qt, merged, out, fq,
-    stage, plane_m, total_m, late_stage, late_plane, deep_p, full_p, natural_p,
+    nd, nz, gt_hbm, tok_hbm, err_hbm, qt_hbm, fq, merged, left_side, right_side,
+    gt, tok, err, qt,
+    stage, plane_m, total_m, late_stage, late_plane, deep_p, late_p, full_p, natural_p,
     part_u, plane_u, full_u,
-    load_sem, ring_send, ring_recv, send_sem, recv_sem, store_sem,
+    load_sem, ring_send, ring_recv, send_sem, recv_sem,
 ):
     dp = lax.axis_index("dp")
     z = lax.axis_index("tensor")
@@ -146,39 +146,47 @@
             parts.append(part.reshape(nd, own, width))
         return parts
 
-    def batch_of(step):
-        return step * BATCHES // half
-
     slots = {}
     for step in range(half):
         for block in ((0,) if step == 0 else (step, -step)):
-            batch = batch_of(step)
+            batch = step
             slots[block] = (batch, sum(1 for b in slots.values() if b[0] == batch))
-    counts = [sum(1 for b in slots.values() if b[0] == k) for k in range(BATCHES)]
-    starts = [sum(counts[:k]) for k in range(BATCHES)]
+    counts = [sum(1 for b in slots.values() if b[0] == k) for k in range(half)]
+    starts = [sum(counts[:k]) for k in range(half)]
+
+    pending = []
+
+    def send_rows(batch, span, offset):
+        there = (
+            lax.rem(place[0] + offset[0], across) * across
+            + lax.rem(place[1] + offset[1], across)
+        ) * 2 + lax.rem(place[2] + offset[2], 2)
+        pltpu.make_async_remote_copy(
+            src_ref=stage.at[there, span],
+            dst_ref=plane_m.at[dp, span],
+            send_sem=send_sem.at[5 + batch],
+            recv_sem=recv_sem.at[5 + batch],
+            device_id={"dp": there},
+            device_id_type=MESH,
+        ).start()
+
+    def send_pending(n):
+        for _ in range(min(n, len(pending))):
+            pending.pop(0)()
 
     def put(step):
         blocks = (0,) if step == 0 else (step, -step)
         for block, part in zip(blocks, multiply(*(at(b) for b in blocks)), strict=True):
             batch, slot = slots[block]
             stage[:, starts[batch] + slot] = part
-        batch = batch_of(step)
-        if step == half - 1 or batch_of(step + 1) != batch:
+        batch = step
+        if True:
             span = pl.ds(starts[batch], counts[batch])
             plane_m[dp, span] = stage[dp, span]
             for offset in far_first:
-                there = (
-                    lax.rem(place[0] + offset[0], across) * across
-                    + lax.rem(place[1] + offset[1], across)
-                ) * 2 + lax.rem(place[2] + offset[2], 2)
-                pltpu.make_async_remote_copy(
-                    src_ref=stage.at[there, span],
-                    dst_ref=plane_m.at[dp, span],
-                    send_sem=send_sem.at[5 + batch],
-                    recv_sem=recv_sem.at[5 + batch],
-                    device_id={"dp": there},
-                    device_id_type=MESH,
-                ).start()
+                pending.append(functools.partial(send_rows, batch, span, offset))
+            if step == half - 1:
+                send_pending(len(pending))
 
     def gather_batch(batch):
         span = pl.ds(starts[batch], counts[batch])
@@ -201,37 +209,55 @@
                 arrived(way, s - 1, piece)
                 if s < half - 1 or (piece < PIECES // 2) == (way == 0):
                     ring(way, s, piece).start()
+            send_pending(nd // PIECES if piece < PIECES - 1 else nd)
         put(s)
-        if s < half - 1 and batch_of(s + 1) != batch_of(s) and batch_of(s) > 0:
-            gather_batch(batch_of(s) - 1)
-    gather_batch(BATCHES - 2)
+        if s > 1:
+            gather_batch(s - 2)
+    gather_batch(half - 2)
     for piece in range(PIECES):
         arrived(0 if piece < PIECES // 2 else 1, half - 1, piece)
     late_stage[...] = multiply(at(half))[0]
     late_plane[dp] = late_stage[dp]
     exchange_dp(0, lambda there: late_stage.at[there], late_plane)
-    gather_batch(BATCHES - 1)
+
+    hd = nz * hb
+    rows_p = nz * own
+    groups = 128 // rank
+    high = rows_p // groups
+    late_blocks = (half - 1, 1 - half, half)
+    for block in late_blocks:
+        total_m[at(block)] = jnp.zeros((own, width), F32)
+
+    def pack(x):
+        return jnp.concatenate([x[k * high : (k + 1) * high] for k in range(groups)], axis=1)
+
+    def unpack(x):
+        return jnp.concatenate([x[:, k * rank : (k + 1) * rank] for k in range(groups)], axis=0)
+
+    deep_p[z] = pack(dot3(total_m[...].reshape(rows_p, width), q[...], NT))
+    exchange_z(1, deep_p.at[z], deep_p)
+    gather_batch(half - 1)
     landed(0, nd, late_plane)
     total_m[at(half)] = jnp.sum(late_plane[...], axis=0)
-
-    hd = nz * hb
-    rows_p = nz * own
+    late = jnp.concatenate([total_m[at(block)] for block in late_blocks], axis=0)
+    late = dot3(late, q[...], NT)
+    late = [late[k * own : (k + 1) * own] for k in range(3)] + [jnp.zeros((own, 128 - 3 * rank), F32)]
+    late_p[z] = jnp.concatenate(late, axis=1)
+    exchange_z(5 + half, late_p.at[z], late_p)
     m = total_m[...].reshape(rows_p, width)
-    part = dot3(m, q[...], NT)
-    groups = 128 // rank
-    high = rows_p // groups
-    deep_p[z] = jnp.concatenate([part[k * high : (k + 1) * high] for k in range(groups)], axis=1)
-    exchange_z(1, deep_p.at[z], deep_p)
     landed(1, nz, deep_p)
-    packed = jnp.sum(deep_p[...], axis=0)
-
-    def unpack(x):
-        return jnp.concatenate([x[:, k * rank : (k + 1) * rank] for k in range(groups)], axis=0)
-
+    early = unpack(jnp.sum(deep_p[...], axis=0))
+    landed(5 + half, nz, late_p)
+    mine = early
+    for k, block in enumerate(late_blocks):
+        x = late_p[...][:, :, k * rank : (k + 1) * rank]
+        shift = -block % nz
+        x = jnp.concatenate([x[shift:], x[:shift]], axis=0)
+        mine = mine + x.reshape(rows_p, rank)
+    packed = pack(mine)
     full_p[dp] = packed
-    exchange_dp(2, lambda there: full_p.at[dp], full_p)
-
-    ut = dot3(unpack(packed), m, TN)
+
+    ut = dot3(mine, m, TN)
     urows = part_u.shape[1]
     utiles = width // 128
     for i in range(rank // urows):
@@ -239,6 +265,10 @@
             part_u[i * utiles + j] = ut[i * urows : (i + 1) * urows, j * 128 : j * 128 + 128]
     plane_u[dp] = part_u[dp]
     exchange_dp(3, lambda there: part_u.at[there], plane_u)
+    exchange_dp(2, lambda there: full_p.at[dp], full_p)
+    landed(3, nd, plane_u)
+    full_u[dp] = jnp.sum(plane_u[...], axis=0)
+    exchange_dp(4, lambda there: full_u.at[dp], full_u)
     landed(2, nd, full_p)
     for j in range(nd):
         natural_p[:, j * own : (j + 1) * own] = unpack(full_p[j]).reshape(nz, own, rank)
@@ -262,11 +292,29 @@
             x = jnp.where(row_id == k, row, jnp.where(row_id > k, x - column * row, x))
         return x
 
-    landed(3, nd, plane_u)
-    full_u[dp] = jnp.sum(plane_u[...], axis=0)
-    exchange_dp(4, lambda there: full_u.at[dp], full_u)
     x = eliminate(x, 0, rank)
     inverse = x[:, rank:]
+    square = lax.dot_general(inverse, inverse, TN, precision=HIGHEST, preferred_element_type=F32)
+    joint = jnp.concatenate([inverse, square / nd], axis=0)
+    p1, p2 = split2(p)
+    left_side[...] = jnp.concatenate([p1, p1, p2], axis=1)
+    def sent(s, carry):
+        for piece in range(PIECES):
+            for way in range(2):
+                ring(way, s, piece).wait_send()
+        return carry
+
+    lax.fori_loop(0, half - 1, sent, 0)
+    for piece in range(PIECES):
+        ring(0 if piece < PIECES // 2 else 1, half - 1, piece).wait_send()
+    for batch in range(half):
+        rest = plane_m.at[pl.ds(0, nd - 1), pl.ds(starts[batch], counts[batch])]
+        pltpu.make_async_copy(rest, rest, send_sem.at[5 + batch]).wait()
+    left(0, nd, late_plane)
+    left(1, nz, deep_p)
+    left(5 + half, nz, late_p)
+    left(2, nd, full_p)
+    left(3, nd, plane_u)
     landed(4, nd, full_u)
     ut = jnp.concatenate(
         [
@@ -275,47 +323,29 @@
         ],
         axis=0,
     )
-    fqt = lax.dot_general(inverse, ut, NN, precision=HIGHEST, preferred_element_type=F32)
+    both = lax.dot_general(joint, ut, NN, precision=HIGHEST, preferred_element_type=F32)
+    fqt = both[:rank]
     fq[...] = fqt
-    fq_store = pltpu.make_async_copy(fq, fq_hbm, store_sem.at[0])
-    fq_store.start()
-    mix = lax.dot_general(inverse, fqt, TN, precision=HIGHEST, preferred_element_type=F32) / nd
-    p1, p2 = split2(p)
-    m1, m2 = split2(mix)
-    left_side = jnp.concatenate([p1, p1, p2], axis=1)
-    right_side = jnp.concatenate([m1, m2, m1], axis=0)
-    stores = []
-    parts = 4
-    per = nz // parts
-    for g in range(parts):
-        n = per * hb
-        low = lax.dot_general(
-            left_side[g * n : (g + 1) * n], right_side, NN, preferred_element_type=F32
+    m1, m2 = split2(both[rank:])
+    right_side[...] = jnp.concatenate([m1, m2, m1], axis=0)
+    left(4, nd, full_u)
+
+
+def finish(fq, merged, left_side, right_side, fq_hbm, new_hbm, out, store_sem):
+    nz, hb, width = out.shape
+    stores = [pltpu.make_async_copy(fq, fq_hbm, store_sem.at[0])]
+    stores[0].start()
+    per = nz // GROUPS
+    for g in range(GROUPS):
+        low = jnp.dot(
+            left_side[g * per * hb : (g + 1) * per * hb],
+            right_side[...],
+            preferred_element_type=F32,
         )
-        at = pl.ds(g * per, per)
-        out[at] = (merged[at] - low.reshape(per, hb, width)).astype(BF16)
-        store = pltpu.make_async_copy(out.at[at], new_hbm.at[at], store_sem.at[1 + g])
-        store.start()
-        stores.append(store)
-
-    def sent(s, carry):
-        for piece in range(PIECES):
-            for way in range(2):
-                ring(way, s, piece).wait_send()
-        return carry
-
-    lax.fori_loop(0, half - 1, sent, 0)
-    for piece in range(PIECES):
-        ring(0 if piece < PIECES // 2 else 1, half - 1, piece).wait_send()
-    for batch in range(BATCHES):
-        rest = plane_m.at[pl.ds(0, nd - 1), pl.ds(starts[batch], counts[batch])]
-        pltpu.make_async_copy(rest, rest, send_sem.at[5 + batch]).wait()
-    left(0, nd, late_plane)
-    left(1, nz, deep_p)
-    left(2, nd, full_p)
-    left(3, nd, plane_u)
-    left(4, nd, full_u)
-    fq_store.wait()
+        span = pl.ds(g * per, per)
+        out[span] = (merged[span] - low.reshape(per, hb, width)).astype(BF16)
+        stores.append(pltpu.make_async_copy(out.at[span], new_hbm.at[span], store_sem.at[1 + g]))
+        stores[-1].start()
     for store in stores:
         store.wait()
 
@@ -329,20 +359,19 @@
     urows = rank * width // nd // 128
     operands = (grad_out.T, tokens, error_old.reshape(nz, hb, width), power_q.T)
     any_space = pl.BlockSpec(memory_space=pl.ANY)
-    fqt, new = pl.pallas_call(
+    held = pl.pallas_call(
         functools.partial(kernel, nd, nz),
         out_shape=(
-            jax.ShapeDtypeStruct((rank, width), F32),
-            jax.ShapeDtypeStruct((nz, hb, width), BF16),
+            pltpu.VMEM((rank, width), F32),
+            pltpu.VMEM((nz, hb, width), F32),
+            pltpu.VMEM((hd, 3 * rank), BF16),
+            pltpu.VMEM((3 * rank, width), BF16),
         ),
         in_specs=[any_space] * 4,
-        out_specs=(any_space, any_space),
+        out_specs=(pl.BlockSpec(memory_space=pltpu.VMEM),) * 4,
         scratch_shapes=[
             pltpu.VMEM((nz, hb, tok_n), BF16),
             pltpu.VMEM((tok_n, width), BF16),
-            pltpu.VMEM((nz, hb, width), BF16),
-            pltpu.VMEM((rank, width), F32),
-            pltpu.VMEM((nz, hb, width), F32),
             pltpu.VMEM((nz, hb, width), BF16),
             pltpu.VMEM((rank, width), F32),
             pltpu.VMEM((nd, nz - 1, hb // nd, width), F32),
@@ -351,6 +380,7 @@
             pltpu.VMEM((nd, hb // nd, width), F32),
             pltpu.VMEM((nd, hb // nd, width), F32),
             pltpu.VMEM((nz, chunk, 128), F32),
+            pltpu.VMEM((nz, hb // nd, 128), F32),
             pltpu.VMEM((nd, chunk, 128), F32),
             pltpu.VMEM((nz, hb, rank), F32),
             pltpu.VMEM((nd, urows, 128), F32),
@@ -359,14 +389,24 @@
             pltpu.SemaphoreType.DMA((4,)),
             pltpu.SemaphoreType.DMA((2, nz // 2, PIECES)),
             pltpu.SemaphoreType.DMA((2, nz // 2, PIECES)),
-            pltpu.SemaphoreType.DMA((5 + BATCHES,)),
-            pltpu.SemaphoreType.DMA((5 + BATCHES,)),
-            pltpu.SemaphoreType.DMA((5,)),
+            pltpu.SemaphoreType.DMA((6 + nz // 2,)),
+            pltpu.SemaphoreType.DMA((6 + nz // 2,)),
         ],
         compiler_params=pltpu.CompilerParams(
-            collective_id=0, has_side_effects=True, vmem_limit_bytes=48 * 1024 * 1024
+            collective_id=0, has_side_effects=True, vmem_limit_bytes=44 * 1024 * 1024
         ),
     )(*(pltpu.with_memory_space_constraint(a, pltpu.HBM) for a in operands))
+    fqt, new = pl.pallas_call(
+        finish,
+        out_shape=(pltpu.HBM((rank, width), F32), pltpu.HBM((nz, hb, width), BF16)),
+        in_specs=[pl.BlockSpec(memory_space=pltpu.VMEM)] * 4,
+        out_specs=(any_space, any_space),
+        scratch_shapes=[
+            pltpu.VMEM((nz, hb, width), BF16),
+            pltpu.SemaphoreType.DMA((1 + GROUPS,)),
+        ],
+        compiler_params=pltpu.CompilerParams(vmem_limit_bytes=8 * 1024 * 1024),
+    )(*(pltpu.with_memory_space_constraint(a, pltpu.VMEM) for a in held))
     return fqt.T, new.reshape(1, hd, width)
 
 

time: 91.8 us -> 87.1 us (0.949)
  Pallas kernels: 89.4 us -> 86.3 us
  local copies, waits for them, and re-layouts: 1.6 us -> 0 us
    pallas_call x1 -> x2, Pallas kernels: 89.4 us -> 86.3 us  [the longest x1 85.1 us: local(): pl.pallas_call(functools.partial(kernel, nd, nz), out_shape=(pltpu.VMEM((...]
    unnamed x2 -> x0, local copies, waits for them, and re-layouts: 1.6 us -> none
where the time goes in v4:
time: 87.1 us; the launch traced here: 87 us
  Pallas kernels  86.3 us (99%)
    pallas_call x1, Pallas kernels, local(): pl.pallas_call(functools.partial(kernel, nd, nz), out_shape=(pltpu.VMEM((...  85.1 us

profile of v4, /device:TPU:1, one launch (start us, length us, event | category | flops | bytes accessed | tf_op | source)
XLA Modules:
  0.0 87.0 jit_solution(5046485940427529851)
XLA Ops:
  0.6 85.1 %shard_map.59 = (f32[32,512]{1,0:T(8,128)S(1)}, f32[16,64,512]{2,1,0:T(8,128)S(1)}, bf16[1024,96]{1,0:T(8,128)(2,1)S(1)}, bf16[96,512]{1,0:T(8,128)(2,1)S(1)}) custom-call(bf16[64,2048]{1,0:T(8,128)(2,1)} %bitcast.6, bf16[2048,512]{1,0:T(8,128)(2,1)} %tok_hbm.1, bf16[16,64,512]{2,1,0:T(8,128)(2,1)} %bitcast.5, f32[32,512]{1,0:T(8,128)} %bitcast.7), custom_call_target="tpu_custom_call" | custom-call | tf_op jit(solution)/shard_map/pallas_call | solution.py:362
  85.8 1.2 %shard_map.60 = (f32[32,512]{1,0:T(8,128)}, bf16[16,64,512]{2,1,0:T(8,128)(2,1)}) custom-call(f32[32,512]{1,0:T(8,128)S(1)} %get-tuple-element.8.fq, f32[16,64,512]{2,1,0:T(8,128)S(1)} %get-tuple-element.9.merged, bf16[1024,96]{1,0:T(8,128)(2,1)S(1)} %get-tuple-element.10.left_side, bf16[96,512]{1,0:T(8,128)(2,1)S(1)} %get-tuple-element.11.right_side), custom_call_target="tpu_custom_call" | custom-call | tf_op jit(solution)/shard_map/pallas_call | solution.py:399

commit v5 on v4

--- a/solution.py
+++ b/solution.py
@@ -26,7 +26,7 @@
 
 def dot3(a, b, dims):
     a1, a2 = split2(a)
-    b1, b2 = split2(b)
+    b1, b2 = b if isinstance(b, tuple) else split2(b)
     dot = functools.partial(lax.dot_general, dimension_numbers=dims, preferred_element_type=F32)
     return dot(a1, b1) + (dot(a1, b2) + dot(a2, b1))
 
@@ -34,7 +34,7 @@
 def kernel(
     nd, nz, gt_hbm, tok_hbm, err_hbm, qt_hbm, fq, merged, left_side, right_side,
     gt, tok, err, qt,
-    stage, plane_m, total_m, late_stage, late_plane, deep_p, late_p, full_p, natural_p,
+    stage, plane_m, total_m, late_part, late_land, deep_p, late_p, full_p, natural_p,
     part_u, plane_u, full_u,
     load_sem, ring_send, ring_recv, send_sem, recv_sem,
 ):
@@ -51,31 +51,27 @@
     offsets = [(i, j, k) for i in range(across) for j in range(across) for k in range(2)][1:]
     far_first = sorted(offsets, key=lambda o: -sum(min(v, across - v) for v in o[:2]))
 
+    def peer(offset):
+        x, y, core = ((p + o) & (n - 1) for p, o, n in zip(place, offset, (across, across, 2)))
+        return (x * across + y) * 2 + core
+
     loads = [
         pltpu.make_async_copy(gt_hbm, gt.at[z], load_sem.at[0]),
         pltpu.make_async_copy(tok_hbm, tok, load_sem.at[1]),
         pltpu.make_async_copy(err_hbm, err, load_sem.at[2]),
         pltpu.make_async_copy(qt_hbm, qt, load_sem.at[3]),
     ]
-    for load in loads:
-        load.start()
+    loads[0].start()
 
     barrier = pltpu.get_barrier_semaphore()
-
-    def greet(axis, n, me):
-        def body(k, carry):
-            pl.semaphore_signal(
-                barrier, inc=1, device_id={axis: lax.rem(me + k, n)}, device_id_type=MESH
-            )
-            return carry
-
-        lax.fori_loop(1, n, body, 0)
-
     for step in (1, nz - 1):
         pl.semaphore_signal(
             barrier, inc=1, device_id={"tensor": lax.rem(z + step, nz)}, device_id_type=MESH
         )
-    greet("dp", nd, dp)
+    for offset in far_first:
+        pl.semaphore_signal(barrier, inc=1, device_id={"dp": peer(offset)}, device_id_type=MESH)
+    for load in loads[1:]:
+        load.start()
     pl.semaphore_wait(barrier, nd + 1)
 
     def ring(way, step, piece):
@@ -100,10 +96,7 @@
 
     def exchange_dp(sems, source, target):
         for offset in far_first:
-            there = (
-                lax.rem(place[0] + offset[0], across) * across
-                + lax.rem(place[1] + offset[1], across)
-            ) * 2 + lax.rem(place[2] + offset[2], 2)
+            there = peer(offset)
             pltpu.make_async_remote_copy(
                 src_ref=source(there),
                 dst_ref=target.at[dp],
@@ -148,7 +141,7 @@
 
     slots = {}
     for step in range(half):
-        for block in ((0,) if step == 0 else (step, -step)):
+        for block in (0,) if step == 0 else (step, -step) + (half,) * (step == half - 1):
             batch = step
             slots[block] = (batch, sum(1 for b in slots.values() if b[0] == batch))
     counts = [sum(1 for b in slots.values() if b[0] == k) for k in range(half)]
@@ -157,10 +150,7 @@
     pending = []
 
     def send_rows(batch, span, offset):
-        there = (
-            lax.rem(place[0] + offset[0], across) * across
-            + lax.rem(place[1] + offset[1], across)
-        ) * 2 + lax.rem(place[2] + offset[2], 2)
+        there = peer(offset)
         pltpu.make_async_remote_copy(
             src_ref=stage.at[there, span],
             dst_ref=plane_m.at[dp, span],
@@ -179,14 +169,11 @@
         for block, part in zip(blocks, multiply(*(at(b) for b in blocks)), strict=True):
             batch, slot = slots[block]
             stage[:, starts[batch] + slot] = part
-        batch = step
-        if True:
-            span = pl.ds(starts[batch], counts[batch])
+        if step < half - 1:
+            span = pl.ds(starts[step], counts[step])
             plane_m[dp, span] = stage[dp, span]
             for offset in far_first:
-                pending.append(functools.partial(send_rows, batch, span, offset))
-            if step == half - 1:
-                send_pending(len(pending))
+                pending.append(functools.partial(send_rows, step, span, offset))
 
     def gather_batch(batch):
         span = pl.ds(starts[batch], counts[batch])
@@ -213,18 +200,28 @@
         put(s)
         if s > 1:
             gather_batch(s - 2)
-    gather_batch(half - 2)
+    late_blocks = (half - 1, 1 - half, half)
+    q_parts = split2(q[...])
+    late = [dot3(merged[at(block)], q_parts, NT) for block in late_blocks[:2]]
     for piece in range(PIECES):
         arrived(0 if piece < PIECES // 2 else 1, half - 1, piece)
-    late_stage[...] = multiply(at(half))[0]
-    late_plane[dp] = late_stage[dp]
-    exchange_dp(0, lambda there: late_stage.at[there], late_plane)
+    part = multiply(at(half))[0]
+    late.append(dot3(merged[at(half)], q_parts, NT))
+    late = [x.reshape(nd, own, rank) for x in late] + [jnp.zeros((nd, own, 128 - 3 * rank), F32)]
+    late_part[...] = jnp.concatenate(late, axis=2)
+    late_land[dp] = late_part[dp]
+    exchange_dp(0, lambda there: late_part.at[there], late_land)
+    stage[:, starts[half - 1] + 2] = part
+    span = pl.ds(starts[half - 1], counts[half - 1])
+    plane_m[dp, span] = stage[dp, span]
+    for offset in far_first:
+        send_rows(half - 1, span, offset)
+    gather_batch(half - 2)
 
     hd = nz * hb
     rows_p = nz * own
     groups = 128 // rank
     high = rows_p // groups
-    late_blocks = (half - 1, 1 - half, half)
     for block in late_blocks:
         total_m[at(block)] = jnp.zeros((own, width), F32)
 
@@ -234,17 +231,13 @@
     def unpack(x):
         return jnp.concatenate([x[:, k * rank : (k + 1) * rank] for k in range(groups)], axis=0)
 
-    deep_p[z] = pack(dot3(total_m[...].reshape(rows_p, width), q[...], NT))
+    deep_p[z] = pack(dot3(total_m[...].reshape(rows_p, width), q_parts, NT))
     exchange_z(1, deep_p.at[z], deep_p)
+    landed(0, nd, late_land)
+    late_p[z] = jnp.sum(late_land[...], axis=0)
+    exchange_z(5 + half, late_p.at[z], late_p)
     gather_batch(half - 1)
-    landed(0, nd, late_plane)
-    total_m[at(half)] = jnp.sum(late_plane[...], axis=0)
-    late = jnp.concatenate([total_m[at(block)] for block in late_blocks], axis=0)
-    late = dot3(late, q[...], NT)
-    late = [late[k * own : (k + 1) * own] for k in range(3)] + [jnp.zeros((own, 128 - 3 * rank), F32)]
-    late_p[z] = jnp.concatenate(late, axis=1)
-    exchange_z(5 + half, late_p.at[z], late_p)
-    m = total_m[...].reshape(rows_p, width)
+    m = split2(total_m[...].reshape(rows_p, width))
     landed(1, nz, deep_p)
     early = unpack(jnp.sum(deep_p[...], axis=0))
     landed(5 + half, nz, late_p)
@@ -310,7 +303,7 @@
     for batch in range(half):
         rest = plane_m.at[pl.ds(0, nd - 1), pl.ds(starts[batch], counts[batch])]
         pltpu.make_async_copy(rest, rest, send_sem.at[5 + batch]).wait()
-    left(0, nd, late_plane)
+    left(0, nd, late_land)
     left(1, nz, deep_p)
     left(5 + half, nz, late_p)
     left(2, nd, full_p)
@@ -374,11 +367,11 @@
             pltpu.VMEM((tok_n, width), BF16),
             pltpu.VMEM((nz, hb, width), BF16),
             pltpu.VMEM((rank, width), F32),
-            pltpu.VMEM((nd, nz - 1, hb // nd, width), F32),
-            pltpu.VMEM((nd, nz - 1, hb // nd, width), F32),
+            pltpu.VMEM((nd, nz, hb // nd, width), F32),
+            pltpu.VMEM((nd, nz, hb // nd, width), F32),
             pltpu.VMEM((nz, hb // nd, width), F32),
-            pltpu.VMEM((nd, hb // nd, width), F32),
-            pltpu.VMEM((nd, hb // nd, width), F32),
+            pltpu.VMEM((nd, hb // nd, 128), F32),
+            pltpu.VMEM((nd, hb // nd, 128), F32),
             pltpu.VMEM((nz, chunk, 128), F32),
             pltpu.VMEM((nz, hb // nd, 128), F32),
             pltpu.VMEM((nd, chunk, 128), F32),

time: 87.1 us -> 86.3 us (level)
  no operation moved by 1% of the time
where the time goes in v5:
time: 86.3 us; the launch traced here: 86.2 us
  Pallas kernels  85.6 us (99%)
    pallas_call x1, Pallas kernels, local(): pl.pallas_call(functools.partial(kernel, nd, nz), out_shape=(pltpu.VMEM((...  84.3 us

profile of v5, /device:TPU:1, one launch (start us, length us, event | category | flops | bytes accessed | tf_op | source)
XLA Modules:
  0.0 86.2 jit_solution(6765588782633529773)
XLA Ops:
  0.6 84.3 %shard_map.59 = (f32[32,512]{1,0:T(8,128)S(1)}, f32[16,64,512]{2,1,0:T(8,128)S(1)}, bf16[1024,96]{1,0:T(8,128)(2,1)S(1)}, bf16[96,512]{1,0:T(8,128)(2,1)S(1)}) custom-call(bf16[64,2048]{1,0:T(8,128)(2,1)} %bitcast.6, bf16[2048,512]{1,0:T(8,128)(2,1)} %tok_hbm.1, bf16[16,64,512]{2,1,0:T(8,128)(2,1)} %bitcast.5, f32[32,512]{1,0:T(8,128)} %bitcast.7), custom_call_target="tpu_custom_call" | custom-call | tf_op jit(solution)/shard_map/pallas_call | solution.py:355
  85.0 1.2 %shard_map.60 = (f32[32,512]{1,0:T(8,128)}, bf16[16,64,512]{2,1,0:T(8,128)(2,1)}) custom-call(f32[32,512]{1,0:T(8,128)S(1)} %get-tuple-element.8.fq, f32[16,64,512]{2,1,0:T(8,128)S(1)} %get-tuple-element.9.merged, bf16[1024,96]{1,0:T(8,128)(2,1)S(1)} %get-tuple-element.10.left_side, bf16[96,512]{1,0:T(8,128)(2,1)S(1)} %get-tuple-element.11.right_side), custom_call_target="tpu_custom_call" | custom-call | tf_op jit(solution)/shard_map/pallas_call | solution.py:392

commit v6 on v5

--- a/solution.py
+++ b/solution.py
@@ -247,8 +247,6 @@
         shift = -block % nz
         x = jnp.concatenate([x[shift:], x[:shift]], axis=0)
         mine = mine + x.reshape(rows_p, rank)
-    packed = pack(mine)
-    full_p[dp] = packed
 
     ut = dot3(mine, m, TN)
     urows = part_u.shape[1]
@@ -258,6 +256,7 @@
             part_u[i * utiles + j] = ut[i * urows : (i + 1) * urows, j * 128 : j * 128 + 128]
     plane_u[dp] = part_u[dp]
     exchange_dp(3, lambda there: part_u.at[there], plane_u)
+    full_p[dp] = pack(mine)
     exchange_dp(2, lambda there: full_p.at[dp], full_p)
     landed(3, nd, plane_u)
     full_u[dp] = jnp.sum(plane_u[...], axis=0)

time: 86.3 us -> 86.3 us (level)
  no operation moved by 1% of the time
where the time goes in v6:
time: 86.3 us; the launch traced here: 86.2 us
  Pallas kernels  85.6 us (99%)
    pallas_call x1, Pallas kernels, local(): pl.pallas_call(functools.partial(kernel, nd, nz), out_shape=(pltpu.VMEM((...  84.3 us

profile of v6, /device:TPU:1, one launch (start us, length us, event | category | flops | bytes accessed | tf_op | source)
XLA Modules:
  0.0 86.2 jit_solution(14386193675381134235)
XLA Ops:
  0.6 84.3 %shard_map.59 = (f32[32,512]{1,0:T(8,128)S(1)}, f32[16,64,512]{2,1,0:T(8,128)S(1)}, bf16[1024,96]{1,0:T(8,128)(2,1)S(1)}, bf16[96,512]{1,0:T(8,128)(2,1)S(1)}) custom-call(bf16[64,2048]{1,0:T(8,128)(2,1)} %bitcast.6, bf16[2048,512]{1,0:T(8,128)(2,1)} %tok_hbm.1, bf16[16,64,512]{2,1,0:T(8,128)(2,1)} %bitcast.5, f32[32,512]{1,0:T(8,128)} %bitcast.7), custom_call_target="tpu_custom_call" | custom-call | tf_op jit(solution)/shard_map/pallas_call | solution.py:354
  85.0 1.2 %shard_map.60 = (f32[32,512]{1,0:T(8,128)}, bf16[16,64,512]{2,1,0:T(8,128)(2,1)}) custom-call(f32[32,512]{1,0:T(8,128)S(1)} %get-tuple-element.8.fq, f32[16,64,512]{2,1,0:T(8,128)S(1)} %get-tuple-element.9.merged, bf16[1024,96]{1,0:T(8,128)(2,1)S(1)} %get-tuple-element.10.left_side, bf16[96,512]{1,0:T(8,128)(2,1)S(1)} %get-tuple-element.11.right_side), custom_call_target="tpu_custom_call" | custom-call | tf_op jit(solution)/shard_map/pallas_call | solution.py:391
